TPU v7x, 32 devices: a whole 2x2x4 slice. The times are simulated.
32 devices in a mesh: dp: 16 (over z, y, x), proto: 2 (over core).
Axes of the slice: x: 2, y: 2, z: 4, core: 2. Of those that a mesh axis runs over, the one named last changes fastest.
Arguments:
- teacher_feats: bfloat16 [8192, 256], P('dp'), may hold values from -0.5 to 0.5
- student_feats: bfloat16 [8192, 256], P('dp'), may hold values from -0.5 to 0.5
- teacher_protos: bfloat16 [32768, 256], P('proto'), may hold values from -0.5 to 0.5
- student_protos: bfloat16 [32768, 256], P('proto'), may hold values from -0.5 to 0.5
Outputs:
- proto_grad: float32 [32768, 256], P(('proto', 'dp'))
- feature_grad: float32 [8192, 256], P('dp')
All inputs are finite; a program needn't handle non-finite values.
Results may differ from a plain program's by a relative error of at most 0.0022.
Values may be sent and summed in bfloat16 or wider, within the bound.
A program may use at most 256 MiB of HBM per device.

v0:
```python
import math

import jax
import jax.numpy as jnp
from jax import lax
from jax.sharding import PartitionSpec as P

ITERS = 3


teacher_temp = 0.07
student_temp = 0.1
norm_eps = 1e-06


def unit_rows(value):
    wide = value.astype(jnp.float32)
    factor = lax.rsqrt(jnp.sum(wide * wide, axis=-1, keepdims=True) + norm_eps)
    return (wide * factor, factor, wide)


def scores(left, right, temp):
    prod = lax.dot_general(
        left, right, (((1,), (1,)), ((), ())), preferred_element_type=jnp.float32
    )
    return jnp.exp(prod / temp)


def shards(teacher_feats, student_feats, teacher_protos, student_protos):
    img_local = teacher_feats.shape[0]
    proto_local = teacher_protos.shape[0]
    images_all = img_local * lax.axis_size("dp")
    protos_all = proto_local * lax.axis_size("proto")
    t_unit, _, _ = unit_rows(teacher_feats)
    t_dir = t_unit.astype(jnp.bfloat16)
    s_unit, s_fac, s_wide = unit_rows(student_feats)
    s_dir = s_unit.astype(jnp.bfloat16)
    tw_unit, _, _ = unit_rows(teacher_protos)
    t_w = tw_unit.astype(jnp.bfloat16)
    sw_unit, _, _ = unit_rows(student_protos)
    s_w = sw_unit.astype(jnp.bfloat16)
    expo_t = scores(t_dir, t_w, teacher_temp)
    expo_s = scores(s_dir, s_w, student_temp)
    student_part = jnp.sum(expo_s, axis=1)
    totals = lax.psum(student_part, "proto")
    row_scale = jnp.ones((img_local,), jnp.float32)
    proto_scale = jnp.ones((proto_local,), jnp.float32)
    for step in range(ITERS):
        col = lax.psum(jnp.sum(expo_t * row_scale[:, None], axis=0), "dp")
        proto_scale = 1.0 / col
        row_part = jnp.sum(expo_t * proto_scale, axis=1)
        rows = lax.psum(row_part, "proto")
        row_scale = 1.0 / rows
    targets = expo_t * proto_scale * row_scale[:, None]
    probs = expo_s * (1.0 / totals)[:, None]
    diff = (probs - targets).astype(jnp.bfloat16)
    feat_part = jnp.dot(diff, s_w, preferred_element_type=jnp.float32)
    feat_sum = lax.psum(feat_part, "proto")
    gz = feat_sum * (math.sqrt(protos_all) / student_temp)
    feature_grad = s_fac * gz - s_wide * (s_fac * s_fac * s_fac) * jnp.sum(
        s_wide * gz, axis=-1, keepdims=True
    )
    rows_out = proto_local // lax.axis_size("dp")
    summed = lax.psum_scatter(
        lax.dot_general(diff, s_dir, (((0,), (0,)), ((), ())), preferred_element_type=jnp.float32),
        "dp",
        scatter_dimension=0,
        tiled=True,
    )
    gw = summed * (protos_all / (student_temp * math.sqrt(images_all)))
    own_rows = lax.dynamic_slice_in_dim(
        student_protos, lax.axis_index("dp") * rows_out, rows_out, 0
    )
    _, own_fac, own_wide = unit_rows(own_rows)
    proto_grad = own_fac * gw - own_wide * (own_fac * own_fac * own_fac) * jnp.sum(
        own_wide * gw, axis=-1, keepdims=True
    )
    return (proto_grad, feature_grad)


def solution(mesh):
    in_specs = (P("dp", None), P("dp", None), P("proto", None), P("proto", None))
    out_specs = (P(("proto", "dp"), None), P("dp", None))
    return jax.shard_map(shards, mesh=mesh, in_specs=in_specs, out_specs=out_specs, check_vma=False)
```

profile of v0, /device:TPU:9, one launch (start us, length us, event | category | flops | bytes accessed | tf_op | source)
XLA Modules:
  0.0 829.4 jit_solution(4597282175228041876)
XLA Ops:
  7.2 0.0 all-reduce.6.cloned.1.call-start
  7.2 5.2 fusion.3
  12.5 1.1 fusion.15
  13.6 0.0 copy-start
  13.6 17.2 %fusion.28 = (f32[16384]{0:T(1024)}, f32[512,16384]{1,0:T(8,128)}) fusion(bf16[16384,256]{1,0:T(8,128)(2,1)} %param.6, f32[16384]{0:T(1024)S(1)} %add_rsqrt_fusion, bf16[512,256]{1,0:T(8,128)(2,1)} %param.4, f32[512]{0:T(512)S(1)} %add_rsqrt_fusion.3), kind=kOutput, calls=%fused_computation.58 | convolution fusion | flops 4324704256 | bytes 42338304 | tf_op jit(solution)/shard_map/dot_general | solution.py:23
  30.8 0.0 all-reduce.6.cloned.1.call-update
  30.8 0.0 all-reduce.8.cloned.1.call-start
  30.9 5.2 fusion.1
  36.1 0.0 copy-done
  36.2 0.1 fusion.17
  36.3 95.1 %all-reduce.6.cloned.1.call-done = f32[16384]{0:T(1024)} async-done(((f32[16384]{0:T(1024)}), f32[16384]{0:T(1024)}) %all-reduce.6.cloned.1.call-update) | async-done | bytes 65552 | tf_op jit(solution)/shard_map/psum | solution.py:49
  131.5 0.9 broadcast_divide_fusion.2
  132.3 12.2 %multiply_reduce_fusion.3 = f32[512]{0:T(512)S(1)} fusion(f32[512,16384]{1,0:T(8,128)} %get-tuple-element.12, f32[16384]{0:T(1024)S(1)} %broadcast_divide_fusion.2), kind=kLoop, calls=%fused_computation.4 | loop fusion | flops 16776704 | bytes 33622016 | tf_op jit(solution)/shard_map/reduce_sum | solution.py:51
  144.5 4.8 psum.58
  149.3 13.2 %multiply_reduce_fusion.2 = f32[16384]{0:T(1024)} fusion(f32[512,16384]{1,0:T(8,128)} %get-tuple-element.12, f32[512]{0:T(512)S(1)} %broadcast_divide_fusion.5), kind=kLoop, calls=%fused_computation.3 | loop fusion | flops 16760832 | bytes 33622016 | tf_op jit(solution)/shard_map/reduce_sum | solution.py:49
  162.6 0.0 all-reduce.8.cloned.1.call-update
  162.6 0.0 all-reduce.10.cloned.1.call-start
  162.7 98.8 %all-reduce.8.cloned.1.call-done = f32[16384]{0:T(1024)} async-done(((f32[16384]{0:T(1024)}), f32[16384]{0:T(1024)}) %all-reduce.8.cloned.1.call-update) | async-done | bytes 65552 | tf_op jit(solution)/shard_map/psum | solution.py:49
  261.4 0.9 broadcast_divide_fusion.1
  262.3 12.2 %multiply_reduce_fusion.1 = f32[512]{0:T(512)S(1)} fusion(f32[512,16384]{1,0:T(8,128)} %get-tuple-element.12, f32[16384]{0:T(1024)S(1)} %broadcast_divide_fusion.1), kind=kLoop, calls=%fused_computation.2 | loop fusion | flops 16776704 | bytes 33622016 | tf_op jit(solution)/shard_map/reduce_sum | solution.py:51
  274.5 4.8 psum.60
  279.3 13.2 %multiply_reduce_fusion = f32[16384]{0:T(1024)} fusion(f32[512,16384]{1,0:T(8,128)} %get-tuple-element.12, f32[512]{0:T(512)S(1)} %broadcast_divide_fusion.4), kind=kLoop, calls=%fused_computation.1 | loop fusion | flops 16760832 | bytes 33622016 | tf_op jit(solution)/shard_map/reduce_sum | solution.py:49
  292.6 0.0 all-reduce.10.cloned.1.call-update
  292.6 0.0 all-reduce.12.cloned.1.call-start
  292.6 16.9 %fusion = (f32[512]{0:T(512)S(1)}, f32[512,16384]{1,0:T(8,128)}) fusion(bf16[16384,256]{1,0:T(8,128)(2,1)} %param.7, f32[16384]{0:T(1024)S(1)} %add_rsqrt_fusion.1, bf16[512,256]{1,0:T(8,128)(2,1)S(1)} %copy-done, f32[512]{0:T(512)S(1)} %get-tuple-element.10), kind=kOutput, calls=%fused_computation.8 | convolution fusion | flops 4324720128 | bytes 42274816 | tf_op jit(solution)/shard_map/dot_general | solution.py:23
  309.6 81.9 %all-reduce.10.cloned.1.call-done = f32[16384]{0:T(1024)} async-done(((f32[16384]{0:T(1024)}), f32[16384]{0:T(1024)}) %all-reduce.10.cloned.1.call-update) | async-done | bytes 65552 | tf_op jit(solution)/shard_map/psum | solution.py:49
  391.4 0.9 broadcast_divide_fusion
  392.3 12.2 %multiply_reduce_fusion.4 = f32[512]{0:T(512)S(1)} fusion(f32[512,16384]{1,0:T(8,128)} %get-tuple-element.12, f32[16384]{0:T(1024)S(1)} %broadcast_divide_fusion), kind=kLoop, calls=%fused_computation.7 | loop fusion | flops 16776704 | bytes 33622016 | tf_op jit(solution)/shard_map/reduce_sum | solution.py:51
  404.5 5.0 all-reduce
  409.5 27.9 %subtract_convert_fusion = bf16[512,16384]{1,0:T(8,128)(2,1)} fusion(f32[512,16384]{1,0:T(8,128)} %get-tuple-element.12, f32[512,16384]{1,0:T(8,128)} %get-tuple-element.14, f32[512]{0:T(512)S(1)} %get-tuple-element.15, f32[16384]{0:T(1024)S(1)} %broadcast_divide_fusion, f32[512]{0:T(512)S(1)} %get-tuple-element.16), kind=kLoop, calls=%fused_computation | loop fusion | flops 50331648 | bytes 83955712 | tf_op jit(solution)/shard_map/convert_element_type | solution.py:56
  437.4 12.9 %fusion.7 = f32[512,256]{1,0:T(8,128)} fusion(bf16[512,16384]{1,0:T(8,128)(2,1)} %subtract_convert_fusion, bf16[16384,256]{1,0:T(8,128)(2,1)} %param.7, f32[16384]{0:T(1024)S(1)} %add_rsqrt_fusion.1), kind=kOutput, calls=%fused_computation.18 | convolution fusion | flops 4307550208 | bytes 25755648 | tf_op jit(solution)/shard_map/dot_general | solution.py:57
  450.2 0.0 all-reduce.12.cloned.1.call-update
  450.2 0.0 reduce-scatter.2.cloned.1.call-start
  450.3 16.2 %fusion.24 = f32[16384,256]{1,0:T(8,128)} fusion(bf16[512,16384]{1,0:T(8,128)(2,1)} %subtract_convert_fusion, bf16[512,256]{1,0:T(8,128)(2,1)S(1)} %copy-done, f32[512]{0:T(512)S(1)} %get-tuple-element.10), kind=kOutput, calls=%fused_computation.41 | convolution fusion | flops 4295360512 | bytes 33818624 | tf_op jit(solution)/shard_map/dot_general | solution.py:65
  466.5 0.0 reduce-scatter.2.cloned.1.call-update
  466.5 2.7 all-reduce.12.cloned.1.call-done
  469.3 1.2 fusion.21
  470.4 2.1 fusion.20
  472.6 345.8 %reduce-scatter.2.cloned.1.call-done = f32[1024,256]{1,0:T(8,128)} async-done(((f32[16384,256]{1,0:T(8,128)}), f32[1024,256]{1,0:T(8,128)}) %reduce-scatter.2.cloned.1.call-update) | async-done | bytes 1048592 | tf_op jit(solution)/shard_map/reduce_scatter | solution.py:64
  818.3 1.7 fusion.11
  820.1 2.8 fusion.13
  (8 shorter events, 0.1 us)
Async XLA Ops:
  7.2 124.3 %all-reduce.6.cloned.1.call-start = ((), (), s32[]{:S(2)}) async-start(), calls=%async_computation.1 | async-start | bytes 131072 | tf_op jit(solution)/shard_map/psum | solution.py:49
  13.6 22.6 %copy-start = (bf16[512,256]{1,0:T(8,128)(2,1)S(1)}, bf16[512,256]{1,0:T(8,128)(2,1)}, u32[]{:S(2)}) copy-start(bf16[512,256]{1,0:T(8,128)(2,1)} %param.5) | copy-start | bytes 786436
  30.8 230.6 %all-reduce.8.cloned.1.call-start = ((), (), s32[]{:S(2)}) async-start(), calls=%async_computation.2 | async-start | bytes 131072 | tf_op jit(solution)/shard_map/psum | solution.py:49
  162.6 228.8 %all-reduce.10.cloned.1.call-start = ((), (), s32[]{:S(2)}) async-start(), calls=%async_computation.3 | async-start | bytes 131072 | tf_op jit(solution)/shard_map/psum | solution.py:49
  292.6 176.7 %all-reduce.12.cloned.1.call-start = ((), (), s32[]{:S(2)}) async-start(), calls=%async_computation.5 | async-start | bytes 1048576 | tf_op jit(solution)/shard_map/psum | solution.py:58
  450.2 368.1 %reduce-scatter.2.cloned.1.call-start = ((), (), s32[]{:S(2)}) async-start(), calls=%async_computation.4 | async-start | bytes 17825792 | tf_op jit(solution)/shard_map/reduce_scatter | solution.py:64
Sparse Core Ops, SparseCore 0:
  31.0 100.4 all-reduce.5
  162.7 98.6 all-reduce.7
  292.7 98.6 all-reduce.9
  450.4 18.8 all-reduce.11
  471.4 346.8 reduce-scatter.1
where the time goes:
time: 836 us; the launch traced here: 829 us
  waiting for transfers between devices  624 us (75%)
  other arithmetic  113 us (14%)
  matrix products  63.2 us (8%)
  blocking collectives  14.5 us (2%)
  between operations  13.9 us (2%)
    reduce_scatter x1, waiting for transfers between devices, shards(): lax.psum_scatter(lax.dot_general(diff, s_dir, (((0,), (0,)), ((), ())), p...  346 us
    psum x3, waiting for transfers between devices, shards(): col = lax.psum(jnp.sum(expo_t * row_scale[:, None], axis=0), 'dp')  276 us
    reduce_sum x3, other arithmetic, shards(): row_part = jnp.sum(expo_t * proto_scale, axis=1)  36.7 us
    dot_general x2, matrix products, scores(): lax.dot_general(left, right, (((1,), (1,)), ((), ())), preferred_element_...  34.2 us
    convert_element_type x1, other arithmetic, shards(): diff = (probs - targets).astype(jnp.bfloat16)  27.9 us
    reduce_sum x2, other arithmetic, shards(): col = lax.psum(jnp.sum(expo_t * row_scale[:, None], axis=0), 'dp')  26.5 us
  transfers between devices with their start and end apart: 5, of which 5 were waited for; matrix products, arithmetic and copies ran while one was open for 5% of the time, Pallas kernels for 0%

commit v1 on v0

v1 whole, which is shorter than its diff:
```python
import functools
import math

import jax
import jax.numpy as jnp
from jax import lax
from jax.experimental import pallas as pl
from jax.experimental.pallas import tpu as pltpu
from jax.sharding import PartitionSpec as P

ITERS = 3
OUTER = 4

teacher_temp = 0.07
student_temp = 0.1
norm_eps = 1e-06
LOG2E = math.log2(math.e)
MESH = pl.DeviceIdType.MESH
f32 = jnp.float32
bf16 = jnp.bfloat16


def dot(a, b, dims):
    return lax.dot_general(a, b, ((dims[:1], dims[1:]), ((), ())), preferred_element_type=f32)


def factor_of(wide):
    return lax.rsqrt(jnp.sum(wide * wide, axis=-1, keepdims=True) + norm_eps)


def unit(value):
    wide = value.astype(f32)
    return (wide * factor_of(wide)).astype(bf16)


def kernel(
    inner, cores, protos_all, images_all,
    tf, sf, tp, sp, out_p, out_f,
    expo, tw, sw, vown, tdir, sdir, sdir_t, rscale, tscale, cacc, tacc, diffs,
    gws, gwr, feat, fxs, fxr, fzs, fzr, fo, colb, psb, rowb,
    lsem, g1s, g1r, g2s, g2r, cs, cr, rs, rr, ws, wr, xs, xr, zs, zr, os_, or_,
):
    block = tf.shape[0]
    strip = block // cores
    images, protos = expo.shape
    rows_out = out_p.shape[0]
    width = min(512, protos)
    chunks = protos // width
    group = OUTER * cores
    d, c = lax.axis_index("dp"), lax.axis_index("proto")
    o, q = d // inner, lax.rem(d, inner)
    g = o * cores + c
    kt, ks = LOG2E / teacher_temp, LOG2E / student_temp

    def col_peer(k):
        return (o * inner + lax.rem(q + k, inner), c)

    def row_peer(k):
        h = lax.rem(g + k, group)
        return ((h // cores) * inner + q, lax.rem(h, cores))

    def z_peer(k):
        return (lax.rem(o + k, OUTER) * inner + q, c)

    def core_peer(j):
        return (d, lax.rem(c + j, cores))

    def from_z(k):
        return lax.rem(o + OUTER - k, OUTER)

    def from_core(j):
        return lax.rem(c + cores - j, cores)

    def aligned(start, size):
        return pl.ds(pl.multiple_of(start, size), size)

    def remote(src, dst, ss, rsm, dev):
        return pltpu.make_async_remote_copy(
            src_ref=src, dst_ref=dst, send_sem=ss, recv_sem=rsm,
            device_id=dev, device_id_type=MESH,
        )

    load_t = pltpu.make_async_copy(tp.at[aligned(o * protos, protos)], tw, lsem.at[0])
    load_s = pltpu.make_async_copy(sp.at[aligned(o * protos, protos)], sw, lsem.at[1])
    load_v = pltpu.make_async_copy(sp.at[aligned(d * rows_out, rows_out)], vown, lsem.at[2])
    load_t.start()
    load_s.start()
    load_v.start()

    barrier = pltpu.get_barrier_semaphore()
    for k in range(1, inner):
        pl.semaphore_signal(barrier, inc=1, device_id=col_peer(k), device_id_type=MESH)
    for k in range(1, group):
        pl.semaphore_signal(barrier, inc=1, device_id=row_peer(k), device_id_type=MESH)
    own = aligned(o * block, block)
    tdir[own, :] = unit(tf[...])
    sdir[own, :] = unit(sf[...])
    pl.semaphore_wait(barrier, inner - 1 + group - 1)

    pending = []

    def strip_rows(buf, ob, part):
        return buf.at[aligned(ob * block + part * strip, strip)]

    def gather_first(n, buf):
        for k in range(1, OUTER):
            part = strip_rows(buf, o, c)
            copy = remote(part, part, g1s.at[n, k], g1r.at[n, k], z_peer(k))
            copy.start()
            pending.append(copy)

    def gather_forward(n, buf):
        for k in range(1, OUTER):
            part = strip_rows(buf, from_z(k), c)
            remote(part, part, g1s.at[n, k], g1r.at[n, k], z_peer(k)).wait_recv()
            for j in range(1, cores):
                copy = remote(part, part, g2s.at[n, k, j], g2r.at[n, k, j], core_peer(j))
                copy.start()
                pending.append(copy)

    def gather_wait(n, buf, k):
        for j in range(1, cores):
            part = strip_rows(buf, from_z(k), from_core(j))
            remote(part, part, g2s.at[n, k, j], g2r.at[n, k, j], core_peer(j)).wait_recv()

    gather_first(0, tdir)
    gather_first(1, sdir)

    def normalize(buf):
        def body(n, _):
            rows = aligned(n * width, width)
            buf[rows, :] = unit(buf[rows, :])
            return 0
        lax.fori_loop(0, chunks, body, 0)

    load_t.wait()
    normalize(tw)

    cacc[...] = jnp.zeros_like(cacc)

    def teacher_block(ob):
        rows = aligned(ob * block, block)

        def body(n, _):
            cols = aligned(n * width, width)
            e = jnp.exp2(dot(tdir[rows, :], tw[cols, :], (1, 1)) * kt)
            expo[rows, cols] = e
            cacc[:, cols] += jnp.sum(e.reshape(block // 8, 8, width), axis=0)
            return 0
        lax.fori_loop(0, chunks, body, 0)

    def student_block(ob):
        rows = aligned(ob * block, block)
        tacc[...] = jnp.zeros_like(tacc)

        def body(n, _):
            cols = aligned(n * width, width)
            e = jnp.exp2(dot(sdir[rows, :], sw[cols, :], (1, 1)) * ks)
            part = e[:, :128]
            for i in range(1, width // 128):
                part += e[:, i * 128:(i + 1) * 128]
            tacc[...] += part
            return 0
        lax.fori_loop(0, chunks, body, 0)
        for i in range(block // 128):
            line = jnp.sum(tacc[i * 128:(i + 1) * 128, :].T, axis=0, keepdims=True)
            rowb[ITERS, 0, pl.ds(ob * (block // 128) + i, 1), :] = line
        sdir_t[:, rows] = sdir[rows, :].T

    def send_cols(it):
        colb[it, 0] = jnp.sum(cacc[...], axis=0, keepdims=True)
        for k in range(1, inner):
            copy = remote(colb.at[it, 0], colb.at[it, k], cs.at[it, k], cr.at[it, k], col_peer(k))
            copy.start()
            pending.append(copy)

    def take_cols(it):
        total = colb[it, 0]
        for k in range(1, inner):
            remote(colb.at[it, 0], colb.at[it, k], cs.at[it, k], cr.at[it, k], col_peer(k)).wait_recv()
            total = total + colb[it, k]
        psb[...] = 1.0 / total

    def send_rows(it):
        for k in range(1, group):
            copy = remote(rowb.at[it, 0], rowb.at[it, k], rs.at[it, k], rr.at[it, k], row_peer(k))
            copy.start()
            pending.append(copy)

    def take_rows(it, dest):
        total = rowb[it, 0]
        for k in range(1, group):
            remote(rowb.at[it, 0], rowb.at[it, k], rs.at[it, k], rr.at[it, k], row_peer(k)).wait_recv()
            total = total + rowb[it, k]
        inv = 1.0 / total
        for i in range(images // 128):
            dest[i * 128:(i + 1) * 128, :] = jnp.broadcast_to(inv[i:i + 1, :], (128, 128)).T

    def row_pass(it):
        def body(rb, _):
            rows = aligned(rb * 128, 128)
            acc = expo[rows, 0:128] * psb[:, 0:128]
            for i in range(1, protos // 128):
                acc += expo[rows, i * 128:(i + 1) * 128] * psb[:, i * 128:(i + 1) * 128]
            rowb[it, 0, pl.ds(rb, 1), :] = jnp.sum(acc.T, axis=0, keepdims=True)
            return 0
        lax.fori_loop(0, images // 128, body, 0)

    def col_pass():
        cacc[...] = jnp.zeros_like(cacc)

        def body(rb, _):
            rows = aligned(rb * 128, 128)
            scale = rscale[rows, :]
            for i in range(protos // 128):
                part = expo[rows, i * 128:(i + 1) * 128] * scale
                cacc[:, i * 128:(i + 1) * 128] += jnp.sum(part.reshape(16, 8, 128), axis=0)
            return 0
        lax.fori_loop(0, images // 128, body, 0)

    teacher_block(o)
    gather_forward(0, tdir)
    for k in range(1, OUTER):
        gather_wait(0, tdir, k)
        teacher_block(from_z(k))
    send_cols(0)
    load_s.wait()
    normalize(sw)
    gather_forward(1, sdir)
    student_block(o)
    fill = 1
    for it in range(ITERS):
        if it > 0:
            col_pass()
            send_cols(it)
            if fill < OUTER:
                gather_wait(1, sdir, fill)
                student_block(from_z(fill))
                fill += 1
                if fill == OUTER:
                    send_rows(ITERS)
            else:
                take_rows(ITERS, tscale)
        take_cols(it)
        row_pass(it)
        send_rows(it)
        if fill < OUTER:
            gather_wait(1, sdir, fill)
            student_block(from_z(fill))
            fill += 1
            if fill == OUTER:
                send_rows(ITERS)
        take_rows(it, rscale)

    def final_chunk(start):
        cols = aligned(start, width)

        def tile(ib, _):
            rows = aligned(ib * block, block)
            es = jnp.exp2(dot(sdir[rows, :], sw[cols, :], (1, 1)) * ks)
            it_, r_ = tscale[rows, :], rscale[rows, :]
            for i in range(width // 128):
                sub = aligned(start + i * 128, 128)
                tgt = expo[rows, sub] * psb[:, sub] * r_
                df = es[:, i * 128:(i + 1) * 128] * it_ - tgt
                diffs[rows, i * 128:(i + 1) * 128] = df.astype(bf16)
            feat[rows, :] += dot(diffs[rows, :], sw[cols, :], (1, 0))
            return 0
        lax.fori_loop(0, OUTER, tile, 0)
        gw_t = dot(sdir_t[...], diffs[...], (1, 0))
        gws[cols, :] = gw_t.T.astype(bf16)

    def gw_copy(k):
        target = lax.rem(q + k, inner)
        return remote(
            gws.at[aligned(target * rows_out, rows_out)], gwr.at[k], ws.at[k], wr.at[k],
            (o * inner + target, c),
        )

    feat[...] = jnp.zeros_like(feat)
    if rows_out % width == 0:
        def per_block(k, _):
            first = lax.rem(q + k, inner) * rows_out

            def inside(s, _):
                final_chunk(first + s * width)
                return 0
            lax.fori_loop(0, rows_out // width, inside, 0)

            @pl.when(k < inner)
            def _():
                gw_copy(k).start()
            return 0
        lax.fori_loop(1, inner + 1, per_block, 0)
    else:
        def per_chunk(n, _):
            final_chunk(n * width)
            return 0
        lax.fori_loop(0, chunks, per_chunk, 0)
        for k in range(1, inner):
            gw_copy(k).start()

    for j in range(1, cores):
        other = lax.rem(c + j, cores)
        for ob in range(OUTER):
            fxs[j, ob * strip:(ob + 1) * strip, :] = feat[aligned(ob * block + other * strip, strip), :].astype(bf16)
        copy = remote(fxs.at[j], fxr.at[j], xs.at[j], xr.at[j], core_peer(j))
        copy.start()
        pending.append(copy)
    for j in range(1, cores):
        remote(fxs.at[j], fxr.at[j], xs.at[j], xr.at[j], core_peer(j)).wait_recv()

    def strip_sum(ob):
        total = feat[aligned(ob * block + c * strip, strip), :]
        for j in range(1, cores):
            total = total + fxr[j, aligned(ob * strip, strip), :].astype(f32)
        return total

    for k in range(1, OUTER):
        fzs[k] = strip_sum(lax.rem(o + k, OUTER)).astype(bf16)
        copy = remote(fzs.at[k], fzr.at[k], zs.at[k], zr.at[k], z_peer(k))
        copy.start()
        pending.append(copy)

    for k in range(1, inner):
        gw_copy(k).wait_recv()
    scale_p = protos_all / (student_temp * math.sqrt(images_all))
    step = min(256, rows_out)

    def proto_rows(n, _):
        rows = aligned(n * step, step)
        gw = gws[aligned(q * rows_out + n * step, step), :].astype(f32)
        for k in range(1, inner):
            gw = gw + gwr[k, rows, :].astype(f32)
        gw = gw * scale_p
        v = vown[rows, :].astype(f32)
        rt = factor_of(v)
        out_p[rows, :] = rt * gw - v * (rt * rt * rt) * jnp.sum(v * gw, axis=-1, keepdims=True)
        return 0
    load_v.wait()
    lax.fori_loop(0, rows_out // step, proto_rows, 0)

    total = strip_sum(o)
    for k in range(1, OUTER):
        remote(fzs.at[k], fzr.at[k], zs.at[k], zr.at[k], z_peer(k)).wait_recv()
        total = total + fzr[k].astype(f32)
    gz = total * (math.sqrt(protos_all) / student_temp)
    mine = aligned(c * strip, strip)
    z = sf[mine, :].astype(f32)
    rt = factor_of(z)
    fo[mine, :] = rt * gz - z * (rt * rt * rt) * jnp.sum(z * gz, axis=-1, keepdims=True)
    for j in range(1, cores):
        part = fo.at[mine]
        copy = remote(part, part, os_.at[j], or_.at[j], core_peer(j))
        copy.start()
        pending.append(copy)
    for j in range(1, cores):
        part = fo.at[aligned(from_core(j) * strip, strip)]
        remote(part, part, os_.at[j], or_.at[j], core_peer(j)).wait_recv()
    out_f[...] = fo[...]
    for k in range(1, inner):
        gw_copy(k).wait_send()
    for copy in pending:
        copy.wait_send()


def shards(teacher_feats, student_feats, teacher_protos, student_protos):
    block, bot = teacher_feats.shape
    proto_local = teacher_protos.shape[0]
    dp, cores = lax.axis_size("dp"), lax.axis_size("proto")
    inner = dp // OUTER
    group = OUTER * cores
    images, protos = block * OUTER, proto_local // OUTER
    rows_out = proto_local // dp
    strip = block // cores
    width = min(512, protos)
    vmem, dma = pltpu.VMEM, pltpu.SemaphoreType.DMA
    scratch = [
        vmem((images, protos), f32),
        vmem((protos, bot), bf16),
        vmem((protos, bot), bf16),
        vmem((rows_out, bot), bf16),
        vmem((images, bot), bf16),
        vmem((images, bot), bf16),
        vmem((bot, images), bf16),
        vmem((images, 128), f32),
        vmem((images, 128), f32),
        vmem((8, protos), f32),
        vmem((block, 128), f32),
        vmem((images, width), bf16),
        vmem((protos, bot), bf16),
        vmem((inner, rows_out, bot), bf16),
        vmem((images, bot), f32),
        vmem((cores, OUTER * strip, bot), bf16),
        vmem((cores, OUTER * strip, bot), bf16),
        vmem((OUTER, strip, bot), bf16),
        vmem((OUTER, strip, bot), bf16),
        vmem((block, bot), f32),
        vmem((ITERS, inner, 1, protos), f32),
        vmem((1, protos), f32),
        vmem((ITERS + 1, group, images // 128, 128), f32),
        dma((3,)),
        dma((2, OUTER)), dma((2, OUTER)),
        dma((2, OUTER, cores)), dma((2, OUTER, cores)),
        dma((ITERS, inner)), dma((ITERS, inner)),
        dma((ITERS + 1, group)), dma((ITERS + 1, group)),
        dma((inner,)), dma((inner,)),
        dma((cores,)), dma((cores,)),
        dma((OUTER,)), dma((OUTER,)),
        dma((cores,)), dma((cores,)),
    ]
    whole = pl.BlockSpec(memory_space=pltpu.VMEM)
    return pl.pallas_call(
        functools.partial(kernel, inner, cores, proto_local * cores, block * dp),
        out_shape=(
            jax.ShapeDtypeStruct((rows_out, bot), f32),
            jax.ShapeDtypeStruct((block, bot), f32),
        ),
        in_specs=[whole, whole, pl.BlockSpec(memory_space=pl.ANY), pl.BlockSpec(memory_space=pl.ANY)],
        out_specs=(whole, whole),
        scratch_shapes=scratch,
        compiler_params=pltpu.CompilerParams(
            collective_id=0, has_side_effects=True, vmem_limit_bytes=63 * 1024 * 1024
        ),
    )(teacher_feats, student_feats, teacher_protos, student_protos)


def solution(mesh):
    in_specs = (P("dp", None), P("dp", None), P("proto", None), P("proto", None))
    out_specs = (P(("proto", "dp"), None), P("dp", None))
    return jax.shard_map(shards, mesh=mesh, in_specs=in_specs, out_specs=out_specs, check_vma=False)
```

time: 836 us -> 123 us (0.15)
  waiting for transfers between devices: 624 us -> 0 us
  Pallas kernels: 0 us -> 118 us
  other arithmetic: 113 us -> 0 us
  matrix products: 63.2 us -> 0 us
  blocking collectives: 14.5 us -> 0 us
  between operations: 13.9 us -> 0.64 us
    reduce_scatter x1 -> x0, waiting for transfers between devices: 346 us -> none  [shards(): lax.psum_scatter(lax.dot_general(diff, s_dir, (((0,), (0,)), ((), ())), p...]
    psum x4 -> x0, waiting for transfers between devices: 279 us -> none  [the longest x3 276 us: shards(): col = lax.psum(jnp.sum(expo_t * row_scale[:, None], axis=0), 'dp')]
    pallas_call x0 -> x1, Pallas kernels: none -> 118 us  [shards(): pl.pallas_call(functools.partial(kernel, inner, cores, proto_local * core...]
    reduce_sum x11 -> x0, other arithmetic: 77.8 us -> none  [the longest x3 36.7 us: shards(): row_part = jnp.sum(expo_t * proto_scale, axis=1)]
    dot_general x4 -> x0, matrix products: 63.2 us -> none  [the longest x2 34.2 us: scores(): lax.dot_general(left, right, (((1,), (1,)), ((), ())), preferred_element_...]
    convert_element_type x1 -> x0, other arithmetic: 27.9 us -> none  [shards(): diff = (probs - targets).astype(jnp.bfloat16)]
    psum x3 -> x0, blocking collectives: 14.5 us -> none  [shards(): rows = lax.psum(row_part, 'proto')]
  transfers between devices with their start and end apart: 5 -> 0, of which waited for: 5 -> 0; matrix products, arithmetic and copies ran while one was open for 5% -> 0% of each run, Pallas kernels for 0% -> 0%
where the time goes in v1:
time: 123 us
  Pallas kernels  118 us (96%)
  local copies, waits for them, and re-layouts  4.13 us (3%)
    pallas_call x1, Pallas kernels, shards(): pl.pallas_call(functools.partial(kernel, inner, cores, proto_local * core...  118 us
    unnamed x2, local copies, waits for them, and re-layouts  4.13 us

profile of v1, /device:TPU:9, one launch (start us, length us, event | category | flops | bytes accessed | tf_op | source)
XLA Modules:
  0.0 122.6 jit_solution(12099062007610947282)
XLA Ops:
  0.6 117.8 %shard_map.59 = (f32[1024,256]{1,0:T(8,128)}, f32[512,256]{1,0:T(8,128)}) custom-call(bf16[512,256]{1,0:T(8,128)(2,1)} %tf.1, bf16[512,256]{1,0:T(8,128)(2,1)} %sf.1, bf16[16384,256]{1,0:T(8,128)(2,1)} %tp.1, bf16[16384,256]{1,0:T(8,128)(2,1)} %sp.1), custom_call_target="tpu_custom_call" | custom-call | tf_op jit(solution)/shard_map/pallas_call | solution.py:413
  118.4 2.3 %copy.8 = f32[1024,256]{1,0:T(8,128)} copy(f32[1024,256]{1,0:T(8,128)} %get-tuple-element.4) | data formatting | bytes 2097152
  120.7 1.9 %copy.9 = f32[512,256]{1,0:T(8,128)} copy(f32[512,256]{1,0:T(8,128)} %get-tuple-element.5) | data formatting | bytes 1048576

commit v2 on v1

--- a/solution.py
+++ b/solution.py
@@ -124,7 +124,6 @@
             remote(part, part, g2s.at[n, k, j], g2r.at[n, k, j], core_peer(j)).wait_recv()
 
     gather_first(0, tdir)
-    gather_first(1, sdir)
 
     def normalize(buf):
         def body(n, _):
@@ -220,6 +219,7 @@
 
     teacher_block(o)
     gather_forward(0, tdir)
+    gather_first(1, sdir)
     for k in range(1, OUTER):
         gather_wait(0, tdir, k)
         teacher_block(from_z(k))
@@ -270,10 +270,14 @@
         gw_t = dot(sdir_t[...], diffs[...], (1, 0))
         gws[cols, :] = gw_t.T.astype(bf16)
 
-    def gw_copy(k):
+    pieces = rows_out // width if rows_out % width == 0 else 1
+    piece = rows_out // pieces
+
+    def gw_copy(k, s):
         target = lax.rem(q + k, inner)
         return remote(
-            gws.at[aligned(target * rows_out, rows_out)], gwr.at[k], ws.at[k], wr.at[k],
+            gws.at[aligned(target * rows_out + s * piece, piece)],
+            gwr.at[k, aligned(s * piece, piece)], ws.at[k, s], wr.at[k, s],
             (o * inner + target, c),
         )
 
@@ -284,12 +288,12 @@
 
             def inside(s, _):
                 final_chunk(first + s * width)
+
+                @pl.when(k < inner)
+                def _():
+                    gw_copy(k, s).start()
                 return 0
-            lax.fori_loop(0, rows_out // width, inside, 0)
-
-            @pl.when(k < inner)
-            def _():
-                gw_copy(k).start()
+            lax.fori_loop(0, pieces, inside, 0)
             return 0
         lax.fori_loop(1, inner + 1, per_block, 0)
     else:
@@ -298,32 +302,39 @@
             return 0
         lax.fori_loop(0, chunks, per_chunk, 0)
         for k in range(1, inner):
-            gw_copy(k).start()
-
-    for j in range(1, cores):
-        other = lax.rem(c + j, cores)
-        for ob in range(OUTER):
-            fxs[j, ob * strip:(ob + 1) * strip, :] = feat[aligned(ob * block + other * strip, strip), :].astype(bf16)
-        copy = remote(fxs.at[j], fxr.at[j], xs.at[j], xr.at[j], core_peer(j))
-        copy.start()
-        pending.append(copy)
-    for j in range(1, cores):
-        remote(fxs.at[j], fxr.at[j], xs.at[j], xr.at[j], core_peer(j)).wait_recv()
-
-    def strip_sum(ob):
+            gw_copy(k, 0).start()
+
+    def fx_copy(j, k):
+        part = pl.ds(k * strip, strip)
+        return remote(fxs.at[j, part], fxr.at[j, part], xs.at[j, k], xr.at[j, k], core_peer(j))
+
+    order = [*range(1, OUTER), 0]
+    for k in order:
+        ob = lax.rem(o + k, OUTER)
+        for j in range(1, cores):
+            other = lax.rem(c + j, cores)
+            fxs[j, k * strip:(k + 1) * strip, :] = feat[aligned(ob * block + other * strip, strip), :].astype(bf16)
+            copy = fx_copy(j, k)
+            copy.start()
+            pending.append(copy)
+
+    def strip_sum(k):
+        ob = lax.rem(o + k, OUTER)
         total = feat[aligned(ob * block + c * strip, strip), :]
         for j in range(1, cores):
-            total = total + fxr[j, aligned(ob * strip, strip), :].astype(f32)
+            fx_copy(j, k).wait_recv()
+            total = total + fxr[j, k * strip:(k + 1) * strip, :].astype(f32)
         return total
 
     for k in range(1, OUTER):
-        fzs[k] = strip_sum(lax.rem(o + k, OUTER)).astype(bf16)
+        fzs[k] = strip_sum(k).astype(bf16)
         copy = remote(fzs.at[k], fzr.at[k], zs.at[k], zr.at[k], z_peer(k))
         copy.start()
         pending.append(copy)
 
     for k in range(1, inner):
-        gw_copy(k).wait_recv()
+        for s in range(pieces):
+            gw_copy(k, s).wait_recv()
     scale_p = protos_all / (student_temp * math.sqrt(images_all))
     step = min(256, rows_out)
 
@@ -340,7 +351,7 @@
     load_v.wait()
     lax.fori_loop(0, rows_out // step, proto_rows, 0)
 
-    total = strip_sum(o)
+    total = strip_sum(0)
     for k in range(1, OUTER):
         remote(fzs.at[k], fzr.at[k], zs.at[k], zr.at[k], z_peer(k)).wait_recv()
         total = total + fzr[k].astype(f32)
@@ -359,7 +370,8 @@
         remote(part, part, os_.at[j], or_.at[j], core_peer(j)).wait_recv()
     out_f[...] = fo[...]
     for k in range(1, inner):
-        gw_copy(k).wait_send()
+        for s in range(pieces):
+            gw_copy(k, s).wait_send()
     for copy in pending:
         copy.wait_send()
 
@@ -374,6 +386,7 @@
     rows_out = proto_local // dp
     strip = block // cores
     width = min(512, protos)
+    pieces = rows_out // width if rows_out % width == 0 else 1
     vmem, dma = pltpu.VMEM, pltpu.SemaphoreType.DMA
     scratch = [
         vmem((images, protos), f32),
@@ -404,8 +417,8 @@
         dma((2, OUTER, cores)), dma((2, OUTER, cores)),
         dma((ITERS, inner)), dma((ITERS, inner)),
         dma((ITERS + 1, group)), dma((ITERS + 1, group)),
-        dma((inner,)), dma((inner,)),
-        dma((cores,)), dma((cores,)),
+        dma((inner, pieces)), dma((inner, pieces)),
+        dma((cores, OUTER)), dma((cores, OUTER)),
         dma((OUTER,)), dma((OUTER,)),
         dma((cores,)), dma((cores,)),
     ]

time: 123 us -> 121 us (0.984)
  Pallas kernels: 118 us -> 116 us
    pallas_call x1, Pallas kernels: 118 us -> 116 us  [shards(): pl.pallas_call(functools.partial(kernel, inner, cores, proto_local * core...]
where the time goes in v2:
time: 121 us; the launch traced here: 120 us
  Pallas kernels  116 us (96%)
  local copies, waits for them, and re-layouts  4.13 us (3%)
    pallas_call x1, Pallas kernels, shards(): pl.pallas_call(functools.partial(kernel, inner, cores, proto_local * core...  116 us
    unnamed x2, local copies, waits for them, and re-layouts  4.13 us

profile of v2, /device:TPU:9, one launch (start us, length us, event | category | flops | bytes accessed | tf_op | source)
XLA Modules:
  0.0 120.4 jit_solution(3625264113589278018)
XLA Ops:
  0.6 115.6 %shard_map.59 = (f32[1024,256]{1,0:T(8,128)}, f32[512,256]{1,0:T(8,128)}) custom-call(bf16[512,256]{1,0:T(8,128)(2,1)} %tf.1, bf16[512,256]{1,0:T(8,128)(2,1)} %sf.1, bf16[16384,256]{1,0:T(8,128)(2,1)} %tp.1, bf16[16384,256]{1,0:T(8,128)(2,1)} %sp.1), custom_call_target="tpu_custom_call" | custom-call | tf_op jit(solution)/shard_map/pallas_call | solution.py:426
  116.2 2.3 %copy.8 = f32[1024,256]{1,0:T(8,128)} copy(f32[1024,256]{1,0:T(8,128)} %get-tuple-element.4) | data formatting | bytes 2097152
  118.5 1.9 %copy.9 = f32[512,256]{1,0:T(8,128)} copy(f32[512,256]{1,0:T(8,128)} %get-tuple-element.5) | data formatting | bytes 1048576
